TPU v7x, 32 devices: a whole 2x2x4 slice. The times are simulated.
32 devices in a mesh: box: 2 (over x), slab: 8 (over z, y), chan: 2 (over core).
Axes of the slice: x: 2, y: 2, z: 4, core: 2. Of those that a mesh axis runs over, the one named last changes fastest.
Arguments:
- field: bfloat16 [64, 128, 4096], P(('box', 'slab'), 'chan'), parts along dimension 0, may hold values from -6 to 6
- conv_one: bfloat16 [3, 3, 3, 128, 128], P(None, None, None, 'chan'), may hold values from -0.109375 to 0.109375
- bias_one: float32 [128], P('chan'), may hold values from -3 to 3
- conv_two: bfloat16 [3, 3, 3, 128, 128], replicated, may hold values from -0.109375 to 0.109375
- bias_two: float32 [128], P('chan'), may hold values from -3 to 3
Outputs:
- block_out: bfloat16 [64, 128, 4096], P(('box', 'slab'), 'chan'), parts along dimension 0
There are 2 independent parts, one for each index of `box`. A program takes and returns all parts, laid end to end along the dimension named above; an argument that names none is the same for every part. Nothing has to cross between parts.
All inputs are finite; a program needn't handle non-finite values.
Results may differ from a plain program's by a relative error of at most 0.0034.
Values may be sent and summed in bfloat16 or wider, within the bound.
A program may use at most 64 MiB of HBM per device.

v0:
```python
import functools

import jax
import jax.numpy as jnp
from jax import lax
from jax.experimental import pallas as pl
from jax.experimental.pallas import tpu as pltpu
from jax.sharding import PartitionSpec as P

SIDE = 64
CELLS = SIDE * SIDE
CHUNKS = 8
ROWS = SIDE // CHUNKS
SPAN = ROWS * SIDE
WIDTH = 128
HALF = WIDTH // 2
MESH = pl.DeviceIdType.MESH


def kernel(
    slabs,
    field, conv_one, conv_two, bias,
    out,
    raw, taps_one, taps_two, raw_one, raw_two, field_wide, hidden_wide, result, biases,
    weight_sem, near_send, near_recv, near_local, far_send, far_recv,
    hidden_send, hidden_recv, out_send, out_recv, out_local,
):
    rank = lax.axis_index("chan")
    slab = lax.axis_index("slab")
    other = 1 - rank
    after = lax.rem(slab + 1, slabs)
    before = lax.rem(slab + slabs - 1, slabs)
    beyond = lax.rem(slab + 2 * rank + slabs - 1, slabs)
    sibling = {"chan": other, "slab": slab}

    barrier = pltpu.get_barrier_semaphore()
    for target in (sibling, {"chan": 0, "slab": beyond}, {"chan": 1, "slab": beyond}):
        pl.semaphore_signal(barrier, inc=1, device_id=target, device_id_type=MESH)

    own = pl.ds(pl.multiple_of(rank * HALF, HALF), HALF)
    theirs = pl.ds(pl.multiple_of(other * HALF, HALF), HALF)

    def part(j):
        return pl.ds(pl.multiple_of(j * SPAN, SPAN), SPAN)

    def remote(src, dst, send, recv, target):
        return pltpu.make_async_remote_copy(
            src_ref=src, dst_ref=dst, send_sem=send, recv_sem=recv,
            device_id=target, device_id_type=MESH,
        )

    def far(j, up):
        plane = 3 if up else 0
        return remote(
            field.at[plane, :, part(j)],
            raw.at[0 if up else 3, own, part(j)],
            far_send.at[0 if up else 1, j],
            far_recv.at[rank, j],
            {"chan": 0, "slab": after} if up else {"chan": 1, "slab": before},
        )

    def near(i):
        return remote(
            field.at[other + i], raw.at[rank + i, own], near_send.at[i], near_recv.at[i], sibling
        )

    def near_own(i):
        return pltpu.make_async_copy(
            field.at[rank + i], raw.at[other + i, own], near_local.at[i]
        )

    send_taps = remote(
        conv_one, raw_one.at[:, own], weight_sem.at[0], weight_sem.at[1], sibling
    )
    send_bias = remote(bias, biases.at[1], weight_sem.at[2], weight_sem.at[3], sibling)
    own_taps = pltpu.make_async_copy(conv_one, raw_one.at[:, own], weight_sem.at[4])
    own_bias = pltpu.make_async_copy(bias, biases.at[0], weight_sem.at[5])
    own_two = pltpu.make_async_copy(conv_two, raw_two, weight_sem.at[6])

    own_taps.start()
    for i in range(3):
        near_own(i).start()
    own_bias.start()
    own_two.start()
    pl.semaphore_wait(barrier, 3)

    send_taps.start()
    send_bias.start()

    def start_far(i):
        j = lax.rem(i + CHUNKS - 1, CHUNKS)
        far(j, True).start()
        far(j, False).start()

    pl.loop(0, CHUNKS)(start_far)
    for i in range(3):
        near(i).start()

    def spread(wide, plane, j, values, centre):
        cells = values.reshape(ROWS, SIDE, WIDTH)
        turned = (pltpu.roll(cells, 1, 1), cells, pltpu.roll(cells, SIDE - 1, 1))
        for c in range(3):
            flat = turned[c].reshape(SPAN, WIDTH).astype(jnp.bfloat16)
            if c != 1 or centre:
                start = pl.multiple_of((j * ROWS + 1) * SIDE, SIDE)
                wide[plane, c, pl.ds(start, SPAN), :] = flat

            @pl.when(j == 0)
            def _():
                wide[plane, c, (SIDE + 1) * SIDE:(SIDE + 2) * SIDE, :] = flat[:SIDE]

            @pl.when(j == CHUNKS - 1)
            def _():
                wide[plane, c, 0:SIDE, :] = flat[SPAN - SIDE:]

    def build(taps, source):
        taps[0:9 * WIDTH, WIDTH:] = jnp.zeros((9 * WIDTH, WIDTH), jnp.bfloat16)
        taps[27 * WIDTH:, :WIDTH] = jnp.zeros((9 * WIDTH, WIDTH), jnp.bfloat16)

        @pl.loop(0, 27)
        def _(t):
            block = source[t].T
            here = pl.multiple_of(t * WIDTH, WIDTH)
            taps[pl.ds(here, WIDTH), :WIDTH] = block
            later = pl.multiple_of((t + 9) * WIDTH, WIDTH)
            taps[pl.ds(later, WIDTH), WIDTH:] = block

    def product(wide, taps, j):
        pieces = []
        for plane in range(4):
            for b in range(3):
                start = pl.multiple_of((j * ROWS + b) * SIDE, SIDE)
                for c in range(3):
                    pieces.append(wide[plane, c, pl.ds(start, SPAN), :])
        return jnp.dot(
            jnp.concatenate(pieces, axis=1), taps[...], preferred_element_type=jnp.float32
        )

    def turn(plane, j):
        values = raw[plane, :, part(j)].astype(jnp.float32).T
        spread(field_wide, plane, j, values, True)

    own_taps.wait()
    send_taps.wait()
    build(taps_one, raw_one)
    own_bias.wait()
    send_bias.wait()

    for i in range(3):
        near_own(i).wait()
        near(i).wait_send()
        pltpu.make_async_remote_copy(
            src_ref=field.at[rank + i], dst_ref=raw.at[other + i, theirs],
            send_sem=near_send.at[i], recv_sem=near_recv.at[i],
            device_id=sibling, device_id_type=MESH,
        ).wait_recv()
        pl.loop(0, CHUNKS)(functools.partial(turn, other + i))

    edge = 3 * rank

    def arrive(j):
        for half in range(2):
            pltpu.make_async_remote_copy(
                src_ref=field.at[0, :, part(j)],
                dst_ref=raw.at[edge, half * HALF:(half + 1) * HALF, part(j)],
                send_sem=far_send.at[half, j], recv_sem=far_recv.at[half, j],
                device_id=sibling, device_id_type=MESH,
            ).wait_recv()
        turn(edge, j)

    down_to = {"chan": other, "slab": lax.rem(slab + rank + slabs - 1, slabs)}
    up_to = {"chan": other, "slab": lax.rem(slab + rank, slabs)}

    def here(j):
        return pl.ds(pl.multiple_of((j * ROWS + 1) * SIDE, SIDE), SPAN)

    def hand(j, up):
        return remote(
            hidden_wide.at[2 if up else 1, 1, here(j)],
            hidden_wide.at[0 if up else 3, 1, here(j)],
            hidden_send.at[0 if up else 1, j],
            hidden_recv.at[0 if up else 1, j],
            up_to if up else down_to,
        )

    def first(j):
        offsets = biases[0, 0:1, :] + biases[1, 0:1, :]
        total = product(field_wide, taps_one, j)
        for z in range(2):
            values = jnp.maximum(total[:, z * WIDTH:(z + 1) * WIDTH] + offsets, 0.0)
            values = values.astype(jnp.bfloat16).astype(jnp.float32)
            spread(hidden_wide, 1 + z, j, values, True)
        hand(j, False).start()
        hand(j, True).start()

    arrive(CHUNKS - 1)
    arrive(0)

    @pl.loop(0, CHUNKS)
    def _(j):
        @pl.when(j < CHUNKS - 2)
        def _():
            arrive(j + 1)

        first(j)

    own_two.wait()
    build(taps_two, raw_two)

    def receive(j):
        for up in (True, False):
            hand(j, up).wait_recv()
            plane = 0 if up else 3
            values = hidden_wide[plane, 1, here(j), :].astype(jnp.float32)
            spread(hidden_wide, plane, j, values, False)

    def give(j):
        return remote(
            result.at[:, theirs, part(j)], out.at[pl.ds(2 * rank, 2), :, part(j)],
            out_send.at[j], out_recv.at[j], sibling,
        )

    def keep(j):
        return pltpu.make_async_copy(
            result.at[:, own, part(j)], out.at[pl.ds(2 * rank, 2), :, part(j)], out_local.at[j]
        )

    def second(j):
        offsets = biases[0, 1:2, :] + biases[1, 1:2, :]
        total = product(hidden_wide, taps_two, j)
        for z in range(2):
            values = total[:, z * WIDTH:(z + 1) * WIDTH] + offsets
            values = values + field_wide[1 + z, 1, here(j), :].astype(jnp.float32)
            values = jnp.maximum(values, 0.0)
            result[z, :, part(j)] = values.T.astype(jnp.bfloat16)
        give(j).start()
        keep(j).start()

    receive(0)
    receive(1)

    @pl.loop(1, CHUNKS + 1)
    def _(j):
        @pl.when(j < CHUNKS - 1)
        def _():
            receive(j + 1)

        second(lax.rem(j, CHUNKS))

    @pl.loop(0, CHUNKS)
    def _(j):
        far(j, True).wait_send()
        far(j, False).wait_send()
        hand(j, True).wait_send()
        hand(j, False).wait_send()
        keep(j).wait()
        give(j).wait_send()
        pltpu.make_async_remote_copy(
            src_ref=result.at[:, theirs, part(j)],
            dst_ref=out.at[pl.ds(2 * other, 2), :, part(j)],
            send_sem=out_send.at[j], recv_sem=out_recv.at[j],
            device_id=sibling, device_id_type=MESH,
        ).wait_recv()


def body(field, conv_one, bias_one, conv_two, bias_two):
    rank = lax.axis_index("chan")
    pair = jnp.stack([bias_one, bias_two])
    own = (jnp.arange(2) == rank)[None, :, None]
    bias = jnp.where(own, pair[:, None, :], 0.0).reshape(2, WIDTH)
    bias = jnp.pad(bias, ((0, 6), (0, 0)))
    anywhere = pl.BlockSpec(memory_space=pl.ANY)
    bf16 = jnp.bfloat16
    padded = (SIDE + 2) * SIDE
    dma = pltpu.SemaphoreType.DMA
    return pl.pallas_call(
        functools.partial(kernel, lax.axis_size("slab")),
        out_shape=jax.ShapeDtypeStruct(field.shape, field.dtype),
        in_specs=[anywhere] * 4,
        out_specs=anywhere,
        scratch_shapes=[
            pltpu.VMEM((4, WIDTH, CELLS), bf16),
            pltpu.VMEM((36 * WIDTH, 2 * WIDTH), bf16),
            pltpu.VMEM((36 * WIDTH, 2 * WIDTH), bf16),
            pltpu.VMEM((27, WIDTH, WIDTH), bf16),
            pltpu.VMEM((27, WIDTH, WIDTH), bf16),
            pltpu.VMEM((4, 3, padded, WIDTH), bf16),
            pltpu.VMEM((4, 3, padded, WIDTH), bf16),
            pltpu.VMEM((2, WIDTH, CELLS), bf16),
            pltpu.VMEM((2, 8, WIDTH), jnp.float32),
            dma((7,)),
            dma((3,)), dma((3,)), dma((3,)),
            dma((2, CHUNKS)), dma((2, CHUNKS)),
            dma((2, CHUNKS)), dma((2, CHUNKS)),
            dma((CHUNKS,)), dma((CHUNKS,)), dma((CHUNKS,)),
        ],
        compiler_params=pltpu.CompilerParams(
            collective_id=0, has_side_effects=True, vmem_limit_bytes=56 * 2**20
        ),
        cost_estimate=pl.CostEstimate(
            flops=2 * 2 * 2 * CELLS * WIDTH * 27 * WIDTH, bytes_accessed=8 * 2**20,
            transcendentals=0,
        ),
    )(field, conv_one.reshape(27, HALF, WIDTH), conv_two.reshape(27, WIDTH, WIDTH), bias)


def solution(mesh):
    return jax.shard_map(
        body,
        mesh=mesh,
        in_specs=(
            P(("box", "slab"), "chan", None),
            P(None, None, None, "chan", None),
            P("chan"),
            P(),
            P("chan"),
        ),
        out_specs=P(("box", "slab"), "chan", None),
        check_vma=False,
    )
```

profile of v0, /device:TPU:0, one launch (start us, length us, event | category | flops | bytes accessed | tf_op | source)
XLA Modules:
  0.0 67.8 jit_solution(11555176270017227501)
XLA Ops:
  0.0 0.1 broadcast_in_dim.28
  0.1 0.1 broadcast_in_dim.29
  0.2 0.7 %pad_maximum_fusion = f32[2,64]{1,0:T(2,128)S(1)} fusion(f32[1,64]{1,0:T(1,128)} %bitcast.4, f32[1,64]{1,0:T(1,128)} %bitcast.5), kind=kLoop, calls=%fused_computation | loop fusion | flops 128 | bytes 1024 | tf_op jit(solution)/shard_map/stack | solution.py:268
  0.9 0.1 broadcast_in_dim.32
  0.9 0.6 pad.4.bias
  1.5 63.1 %shard_map.55 = bf16[4,64,4096]{2,1,0:T(8,128)(2,1)} custom-call(bf16[4,64,4096]{2,1,0:T(8,128)(2,1)} %field.1, bf16[27,64,128]{2,1,0:T(8,128)(2,1)} %bitcast.7, bf16[27,128,128]{2,1,0:T(8,128)(2,1)} %bitcast.6, f32[8,128]{1,0:T(8,128)} %pad.4.bias), custom_call_target="tpu_custom_call" | custom-call | flops 14495514624 | bytes 8388608 | tf_op jit(solution)/shard_map/pallas_call | solution.py:276
  64.6 3.1 %copy.7 = bf16[4,64,4096]{2,1,0:T(8,128)(2,1)} copy(bf16[4,64,4096]{2,1,0:T(8,128)(2,1)} %shard_map.55) | data formatting | bytes 4194304
  (3 shorter events, 0.0 us)
where the time goes:
time: 67.9 us; the launch traced here: 67.8 us
  Pallas kernels  63.1 us (93%)
  local copies, waits for them, and re-layouts  3.98 us (6%)
  other arithmetic  0.69 us (1%)
    pallas_call x1, Pallas kernels, body(): pl.pallas_call(functools.partial(kernel, lax.axis_size('slab')), out_shap...  63.1 us
    unnamed x1, local copies, waits for them, and re-layouts  3.13 us

commit v1 on v0

--- a/solution.py
+++ b/solution.py
@@ -8,6 +8,7 @@
 from jax.sharding import PartitionSpec as P
 
 SIDE = 64
+DEPTH = 4
 CELLS = SIDE * SIDE
 CHUNKS = 8
 ROWS = SIDE // CHUNKS
@@ -92,9 +93,16 @@
         far(j, True).start()
         far(j, False).start()
 
-    pl.loop(0, CHUNKS)(start_far)
+    def end_far(i):
+        j = lax.rem(i + CHUNKS - 1, CHUNKS)
+        far(j, True).wait_send()
+        far(j, False).wait_send()
+
+    start_far(0)
     for i in range(3):
         near(i).start()
+    for i in range(1, DEPTH):
+        start_far(i)
 
     def spread(wide, plane, j, values, centre):
         cells = values.reshape(ROWS, SIDE, WIDTH)
@@ -174,14 +182,24 @@
     def here(j):
         return pl.ds(pl.multiple_of((j * ROWS + 1) * SIDE, SIDE), SPAN)
 
-    def hand(j, up):
+    def lines(m):
+        return pl.ds(pl.multiple_of((m * ROWS + 2) * SIDE, SIDE), SPAN)
+
+    head = pl.ds(ROWS * SIDE, 2 * SIDE)
+    tail = pl.ds(2 * SIDE, (ROWS - 2) * SIDE)
+
+    def hand(m, up, cells):
         return remote(
-            hidden_wide.at[2 if up else 1, 1, here(j)],
-            hidden_wide.at[0 if up else 3, 1, here(j)],
-            hidden_send.at[0 if up else 1, j],
-            hidden_recv.at[0 if up else 1, j],
+            hidden_wide.at[2 if up else 1, 1, cells],
+            hidden_wide.at[0 if up else 3, 1, cells],
+            hidden_send.at[0 if up else 1, m],
+            hidden_recv.at[0 if up else 1, m],
             up_to if up else down_to,
         )
+
+    def hand_both(m, cells):
+        hand(m, False, cells).start()
+        hand(m, True, cells).start()
 
     def first(j):
         offsets = biases[0, 0:1, :] + biases[1, 0:1, :]
@@ -190,10 +208,11 @@
             values = jnp.maximum(total[:, z * WIDTH:(z + 1) * WIDTH] + offsets, 0.0)
             values = values.astype(jnp.bfloat16).astype(jnp.float32)
             spread(hidden_wide, 1 + z, j, values, True)
-        hand(j, False).start()
-        hand(j, True).start()
-
+    end_far(0)
+    start_far(DEPTH)
     arrive(CHUNKS - 1)
+    end_far(1)
+    start_far(DEPTH + 1)
     arrive(0)
 
     @pl.loop(0, CHUNKS)
@@ -201,18 +220,49 @@
         @pl.when(j < CHUNKS - 2)
         def _():
             arrive(j + 1)
+            end_far(j + 2)
+
+            @pl.when(j + 2 + DEPTH < CHUNKS)
+            def _():
+                start_far(j + 2 + DEPTH)
+
+        @pl.when(j == CHUNKS - 4)
+        def _():
+            hand_both(CHUNKS, head)
+            hand_both(1, lines(1))
+
+        @pl.when(j == CHUNKS - 3)
+        def _():
+            pl.loop(2, CHUNKS - 4)(lambda m: hand_both(m, lines(m)))
 
         first(j)
+
+        @pl.when(j >= CHUNKS - 3)
+        def _():
+            hand_both(j - 1, lines(j - 1))
+
+    hand_both(CHUNKS - 1, lines(CHUNKS - 1))
+    hand_both(0, tail)
 
     own_two.wait()
     build(taps_two, raw_two)
 
-    def receive(j):
+    def receive(m, cells, rows):
         for up in (True, False):
-            hand(j, up).wait_recv()
+            hand(m, up, cells).wait_recv()
             plane = 0 if up else 3
-            values = hidden_wide[plane, 1, here(j), :].astype(jnp.float32)
-            spread(hidden_wide, plane, j, values, False)
+            values = hidden_wide[plane, 1, cells, :].astype(jnp.float32)
+            grid = values.reshape(rows, SIDE, WIDTH)
+            turned = (pltpu.roll(grid, 1, 1), grid, pltpu.roll(grid, SIDE - 1, 1))
+            for c in range(3):
+                flat = turned[c].reshape(rows * SIDE, WIDTH).astype(jnp.bfloat16)
+                if c != 1:
+                    hidden_wide[plane, c, cells, :] = flat
+                if rows == ROWS:
+                    @pl.when(m == CHUNKS - 1)
+                    def _():
+                        hidden_wide[plane, c, 0:SIDE, :] = flat[SPAN - 2 * SIDE:SPAN - SIDE]
+                        hidden_wide[plane, c, SIDE:2 * SIDE, :] = flat[SPAN - SIDE:]
 
     def give(j):
         return remote(
@@ -236,23 +286,27 @@
         give(j).start()
         keep(j).start()
 
-    receive(0)
-    receive(1)
+    receive(CHUNKS, head, 2)
 
     @pl.loop(1, CHUNKS + 1)
     def _(j):
-        @pl.when(j < CHUNKS - 1)
-        def _():
-            receive(j + 1)
+        @pl.when(j < CHUNKS)
+        def _():
+            receive(j, lines(j), ROWS)
+
+        @pl.when(j == CHUNKS)
+        def _():
+            receive(0, tail, ROWS - 2)
 
         second(lax.rem(j, CHUNKS))
+
+    for up in (True, False):
+        hand(CHUNKS, up, head).wait_send()
+        hand(0, up, tail).wait_send()
+        pl.loop(1, CHUNKS)(lambda m: hand(m, up, lines(m)).wait_send())
 
     @pl.loop(0, CHUNKS)
     def _(j):
-        far(j, True).wait_send()
-        far(j, False).wait_send()
-        hand(j, True).wait_send()
-        hand(j, False).wait_send()
         keep(j).wait()
         give(j).wait_send()
         pltpu.make_async_remote_copy(
@@ -275,9 +329,9 @@
     dma = pltpu.SemaphoreType.DMA
     return pl.pallas_call(
         functools.partial(kernel, lax.axis_size("slab")),
-        out_shape=jax.ShapeDtypeStruct(field.shape, field.dtype),
+        out_shape=pltpu.VMEM(field.shape, field.dtype),
         in_specs=[anywhere] * 4,
-        out_specs=anywhere,
+        out_specs=pl.BlockSpec(memory_space=pltpu.VMEM),
         scratch_shapes=[
             pltpu.VMEM((4, WIDTH, CELLS), bf16),
             pltpu.VMEM((36 * WIDTH, 2 * WIDTH), bf16),
@@ -291,7 +345,7 @@
             dma((7,)),
             dma((3,)), dma((3,)), dma((3,)),
             dma((2, CHUNKS)), dma((2, CHUNKS)),
-            dma((2, CHUNKS)), dma((2, CHUNKS)),
+            dma((2, CHUNKS + 1)), dma((2, CHUNKS + 1)),
             dma((CHUNKS,)), dma((CHUNKS,)), dma((CHUNKS,)),
         ],
         compiler_params=pltpu.CompilerParams(

time: 67.9 us -> 63.5 us (0.935)
  the two profiles are of different devices: /device:TPU:0 before, /device:TPU:11 now
where the time goes in v1:
time: 63.5 us; the launch traced here: 63.4 us
  Pallas kernels  60.5 us (95%)
  local copies, waits for them, and re-layouts  2.17 us (3%)
  other arithmetic  0.69 us (1%)
    pallas_call x1, Pallas kernels, body(): pl.pallas_call(functools.partial(kernel, lax.axis_size('slab')), out_shap...  60.5 us
    unnamed x1, local copies, waits for them, and re-layouts  1.32 us

profile of v1, /device:TPU:11, one launch (start us, length us, event | category | flops | bytes accessed | tf_op | source)
XLA Modules:
  0.0 63.4 jit_solution(4525237633059773912)
XLA Ops:
  0.0 0.1 broadcast_in_dim.28
  0.1 0.1 broadcast_in_dim.29
  0.2 0.7 %pad_maximum_fusion = f32[2,64]{1,0:T(2,128)S(1)} fusion(f32[1,64]{1,0:T(1,128)} %bitcast.4, f32[1,64]{1,0:T(1,128)} %bitcast.5), kind=kLoop, calls=%fused_computation | loop fusion | flops 128 | bytes 1024 | tf_op jit(solution)/shard_map/stack | solution.py:322
  0.9 0.1 broadcast_in_dim.32
  0.9 0.6 pad.4.bias
  1.5 60.5 %shard_map.55 = bf16[4,64,4096]{2,1,0:T(8,128)(2,1)S(1)} custom-call(bf16[4,64,4096]{2,1,0:T(8,128)(2,1)} %field.1, bf16[27,64,128]{2,1,0:T(8,128)(2,1)} %bitcast.7, bf16[27,128,128]{2,1,0:T(8,128)(2,1)} %bitcast.6, f32[8,128]{1,0:T(8,128)} %pad.4.bias), custom_call_target="tpu_custom_call" | custom-call | flops 14495514624 | bytes 8388608 | tf_op jit(solution)/shard_map/pallas_call | solution.py:330
  62.0 1.3 %copy.7 = bf16[4,64,4096]{2,1,0:T(8,128)(2,1)} copy(bf16[4,64,4096]{2,1,0:T(8,128)(2,1)S(1)} %shard_map.55) | data formatting | bytes 4194304
  (3 shorter events, 0.0 us)
